TPU v7x, 32 devices: a whole 2x2x4 slice. The times are simulated.
32 devices in a mesh: dp: 8 (over z, core), tensor: 4 (over y, x).
Axes of the slice: x: 2, y: 2, z: 4, core: 2. Of those that a mesh axis runs over, the one named last changes fastest.
Arguments:
- embeddings: bfloat16 [8192, 3584], P('dp'), may hold values from -6 to 6
- proj_weight: bfloat16 [3584, 1024], P(None, 'tensor'), may hold values from -0.09375 to 0.09375
- class_prior: float32 [8192, 512], P(('dp', 'tensor')), may hold values from 0.05 to 1
- seed_mask: int32 [8192], P(('dp', 'tensor')), may hold values 0 or 1
- nbr_block: int32 [32, 5], replicated, may hold values from 0 to 31, as said below
- nbr_cols: int32 [8192, 5, 8], P(('dp', 'tensor')), may hold values from 0 to 255
Outputs:
- labels: float32 [8192, 512], P(('dp', 'tensor'))
Inputs may be any that keep to these rules, and one draw needn't show every extreme that they name: `nbr_block`: for row block b, the entries name blocks with the same remainder modulo 4 as b; the quotient by 4 equals that of b plus an offset modulo 8; the first entry's offset is +1, the others are distinct offsets drawn from -3, -2, -1, 2, 3, 4.
All inputs are finite; a program needn't handle non-finite values. No bound on the sum of `seed_mask` on one device may be relied on, other than what follows from the above.
Results may differ from a plain program's by a relative error of at most 0.0012.
Values may be sent and summed in bfloat16 or wider, within the bound.
A program may use at most 128 MiB of HBM per device.

v0:
```python
import jax
import jax.numpy as jnp
from jax import lax
from jax.sharding import PartitionSpec as P

ITERS = 3


eps_norm = 1e-06
beta_scale = 16.0
alpha_keep = 0.8


def pick_columns(onehot_mask, slot_tiles):
    return jnp.sum(jnp.where(onehot_mask, slot_tiles[:, :, None, :], 0.0), axis=3)


def body(embeddings, proj_weight, class_prior, seed_mask, nbr_block, nbr_cols):
    panels = lax.axis_size("tensor")
    tensor_pos = lax.axis_index("tensor")
    data_pos = lax.axis_index("dp")
    block_rows = embeddings.shape[0] // panels
    slot_count = nbr_cols.shape[1]
    pick_count = nbr_cols.shape[2]
    feature_count = proj_weight.shape[1] * panels
    cols_part = jnp.dot(embeddings, proj_weight, preferred_element_type=jnp.float32).astype(
        jnp.bfloat16
    )
    own_panel = lax.all_to_all(cols_part, "tensor", split_axis=0, concat_axis=1, tiled=True)
    panel_f = own_panel.astype(jnp.float32)
    unit_rows = (
        panel_f * lax.rsqrt(jnp.sum(panel_f * panel_f, axis=1, keepdims=True) + eps_norm)
    ).astype(jnp.bfloat16)
    own_block = data_pos * panels + tensor_pos
    own_list = lax.dynamic_slice_in_dim(nbr_block, own_block, 1, 0)[0]
    target_dp = own_list // panels
    column_ids = jnp.arange(block_rows, dtype=jnp.int32)
    onehot_mask = nbr_cols[..., None] == column_ids
    add_shard_rows = lax.all_gather(unit_rows, "dp", axis=0, tiled=True)
    add_group_count = add_shard_rows.shape[0] // block_rows
    pieces = add_shard_rows.reshape(add_group_count, block_rows, feature_count)
    products = jnp.einsum("id,qjd->iqj", unit_rows, pieces, preferred_element_type=jnp.float32)
    add_block_ids = jnp.arange(add_group_count, dtype=jnp.int32)
    add_match = add_block_ids[:, None] == target_dp[None, :]
    slot_tiles = jnp.sum(
        jnp.where(add_match[None, :, :, None], products[:, :, None, :], 0.0), axis=1
    )
    values = pick_columns(onehot_mask, slot_tiles)
    cosine = values.reshape(block_rows, slot_count * pick_count)
    weights = jnp.exp(beta_scale * cosine)
    degree = jnp.sum(weights, axis=1)
    inv_root = lax.rsqrt(degree)[:, None]
    weight_grid = weights.reshape(block_rows, slot_count, pick_count)
    affinity = jnp.transpose(
        jnp.sum(jnp.where(onehot_mask, weight_grid[..., None], 0.0), axis=2), (1, 0, 2)
    ).astype(jnp.bfloat16)
    seed_prior = (
        seed_mask.astype(jnp.float32)[:, None]
        * class_prior
        / jnp.mean(class_prior, axis=1, keepdims=True)
    )
    labels = seed_prior
    for iteration in range(ITERS):
        scaled = (labels * inv_root).astype(jnp.bfloat16)
        shard_rows = lax.all_gather(scaled, "dp", axis=0, tiled=True)
        group_count = shard_rows.shape[0] // block_rows
        block_ids = jnp.arange(group_count, dtype=jnp.int32)
        match = block_ids[:, None] == target_dp[None, :]
        chosen = jnp.where(
            jnp.transpose(match)[:, None, :, None],
            affinity[:, :, None, :],
            jnp.zeros((), jnp.bfloat16),
        )
        combined = jnp.sum(chosen, axis=0).reshape(block_rows, group_count * block_rows)
        spread = jnp.dot(combined, shard_rows, preferred_element_type=jnp.float32)
        labels = alpha_keep * inv_root * spread + (1.0 - alpha_keep) * seed_prior
    return labels


def solution(mesh):
    return jax.shard_map(
        body,
        mesh=mesh,
        in_specs=(
            P("dp", None),
            P(None, "tensor"),
            P(("dp", "tensor"), None),
            P(("dp", "tensor")),
            P(),
            P(("dp", "tensor"), None, None),
        ),
        out_specs=P(("dp", "tensor"), None),
        check_vma=False,
    )
```

profile of v0, /device:TPU:0, one launch (start us, length us, event | category | flops | bytes accessed | tf_op | source)
XLA Modules:
  0.0 198.6 jit_solution(3650592719502322440)
XLA Ops:
  6.5 1.5 copy-done
  8.0 5.1 %convolution_convert_fusion = bf16[1024,256]{1,0:T(8,128)(2,1)S(1)} fusion(bf16[1024,3584]{1,0:T(8,128)(2,1)} %param.6, bf16[3584,256]{1,0:T(8,128)(2,1)S(1)} %copy-done), kind=kOutput, calls=%fused_computation.5 | convolution fusion | flops 1879310336 | bytes 9699328 | tf_op jit(solution)/shard_map/dot_general | solution.py:26
  13.2 0.2 copy.24
  13.4 13.5 %all_to_all.13 = bf16[4,256,256]{1,2,0:T(8,128)(2,1)S(1)} all-to-all(bf16[4,256,256]{1,2,0:T(8,128)(2,1)S(1)} %copy.24), channel_id=1, replica_groups=mesh['dp'=8,'tensor'=4] {'tensor'}, dimensions={0} | all-to-all | bytes 1048576 | tf_op jit(solution)/shard_map/all_to_all | solution.py:29
  26.9 0.2 multiply_reduce_fusion
  27.1 0.9 fusion.7
  28.1 0.4 copy.23
  28.5 1.2 reduce_sum.80
  29.7 0.2 fusion.9
  29.9 0.1 iota_compare_fusion.2
  30.0 0.9 multiply_convert_fusion
  30.9 44.8 %all-gather.5.cloned.1.call-done = bf16[2048,1024]{0,1:T(8,128)(2,1)} async-done(((bf16[256,1024]{0,1:T(8,128)(2,1)}), bf16[2048,1024]{0,1:T(8,128)(2,1)}) %all-gather.5.cloned.1.call-update) | async-done | bytes 4194320 | tf_op jit(solution)/shard_map/all_gather | solution.py:39
  75.7 6.4 %copy.25 = bf16[2048,1024]{1,0:T(8,128)(2,1)} copy(bf16[2048,1024]{0,1:T(8,128)(2,1)} %all-gather.5.cloned.1.call-done) | data formatting | bytes 8388608 | tf_op jit(solution)/shard_map/all_gather | solution.py:39
  82.1 3.5 %fusion.12 = f32[256,8,256]{2,0,1:T(8,128)S(1)} fusion(bf16[256,1024,1]{0,1,2:T(8,128)(2,1)S(1)} %bitcast.34, bf16[8,256,1024]{2,1,0:T(8,128)(2,1)} %bitcast.29), kind=kOutput, calls=%fused_computation.38 | convolution fusion | flops 1073741824 | bytes 6815744 | tf_op jit(solution)/shard_map/id,qjd->iqj/dot_general | solution.py:42
  85.6 1.2 copy.27
  86.8 4.0 %select_reduce_fusion.2 = f32[256,5,256]{2,1,0:T(8,128)S(1)} fusion(f32[256,8,256]{2,1,0:T(8,128)S(1)} %copy.27, pred[8,5]{0,1:T(8,128)(4,1)S(1)} %iota_compare_fusion.2), kind=kLoop, calls=%fused_computation.2 | loop fusion | flops 4915200 | bytes 3407912 | tf_op jit(solution)/shard_map/reduce_sum | solution.py:45
  90.8 4.7 %select_reduce_fusion.1 = f32[256,5,8]{2,1,0:T(8,128)} fusion(f32[256,5,256]{2,1,0:T(8,128)S(1)} %select_reduce_fusion.2, s32[256,5,8]{2,1,0:T(8,128)S(1)} %copy.23), kind=kLoop, calls=%fused_computation.1 | loop fusion | flops 7854080 | bytes 1392640 | tf_op jit(solution)/shard_map/reduce_sum | solution.py:15
  95.5 1.4 copy.28
  96.9 0.9 multiply_convert_fusion.1
  97.8 0.2 all-gather.9.cloned.1.call-start
  98.1 0.1 iota_compare_fusion.1
  98.2 1.3 copy.29
  99.5 5.6 %select_reduce_fusion = bf16[256,5,256]{2,1,0:T(8,128)(2,1)S(1)} fusion(f32[256,5,8]{2,1,0:T(8,128)} %copy.29, s32[256,5,8]{2,1,0:T(8,128)S(1)} %copy.23), kind=kLoop, calls=%fused_computation | loop fusion | flops 7536640 | bytes 737280 | tf_op jit(solution)/shard_map/reduce_sum | solution.py:55
  105.1 0.1 copy.30
  105.2 1.8 select_reduce_fusion.3
  107.0 0.3 copy.33
  107.3 18.0 %all-gather.7.cloned.1.call-done = bf16[2048,512]{1,0:T(8,128)(2,1)} async-done(((bf16[256,512]{1,0:T(8,128)(2,1)}), bf16[2048,512]{1,0:T(8,128)(2,1)}) %all-gather.7.cloned.1.call-update) | async-done | bytes 2097168 | tf_op jit(solution)/shard_map/all_gather | solution.py:65
  125.3 3.0 %fusion.6 = bf16[256,512]{1,0:T(8,128)(2,1)} fusion(bf16[256,2048]{1,0:T(8,128)(2,1)S(1)} %bitcast.31, bf16[2048,512]{1,0:T(8,128)(2,1)} %all-gather.7.cloned.1.call-done, f32[256]{0:T(256)S(1)} %get-tuple-element.8, f32[256]{0:T(256)S(1)} %get-tuple-element.7, f32[256]{0:T(256)S(1)} %get-tuple-element.9, f32[256,512]{1,0:T(8,128)S(1)} %copy-done.1, ...), kind=kOutput, calls=%fused_computation.15 | convolution fusion | flops 537788416 | bytes 3936256 | tf_op jit(solution)/shard_map/dot_general | solution.py:75
  128.4 28.7 %all-gather.9.cloned.1.call-done = bf16[2048,512]{1,0:T(8,128)(2,1)} async-done(((bf16[256,512]{1,0:T(8,128)(2,1)}), bf16[2048,512]{1,0:T(8,128)(2,1)}) %all-gather.9.cloned.1.call-update) | async-done | bytes 2097168 | tf_op jit(solution)/shard_map/all_gather | solution.py:65
  157.1 3.0 %fusion.5 = bf16[256,512]{1,0:T(8,128)(2,1)} fusion(bf16[256,2048]{1,0:T(8,128)(2,1)S(1)} %bitcast.32, bf16[2048,512]{1,0:T(8,128)(2,1)} %all-gather.9.cloned.1.call-done, f32[256]{0:T(256)S(1)} %get-tuple-element.8, f32[256]{0:T(256)S(1)} %get-tuple-element.7, f32[256]{0:T(256)S(1)} %get-tuple-element.9, f32[256,512]{1,0:T(8,128)S(1)} %copy-done.1, ...), kind=kOutput, calls=%fused_computation.14 | convolution fusion | flops 537788416 | bytes 3936256 | tf_op jit(solution)/shard_map/dot_general | solution.py:75
  160.2 28.8 %all-gather.11.cloned.1.call-done = bf16[2048,512]{1,0:T(8,128)(2,1)} async-done(((bf16[256,512]{1,0:T(8,128)(2,1)}), bf16[2048,512]{1,0:T(8,128)(2,1)}) %all-gather.11.cloned.1.call-update) | async-done | bytes 2097168 | tf_op jit(solution)/shard_map/all_gather | solution.py:65
  188.9 3.1 %fusion = f32[256,512]{1,0:T(8,128)} fusion(bf16[256,2048]{1,0:T(8,128)(2,1)S(1)} %bitcast.33, bf16[2048,512]{1,0:T(8,128)(2,1)} %all-gather.11.cloned.1.call-done, f32[256]{0:T(256)S(1)} %get-tuple-element.7, f32[256]{0:T(256)S(1)} %get-tuple-element.9, f32[256,512]{1,0:T(8,128)S(1)} %copy-done.1, f32[256]{0:T(256)S(1)} %convert_element_type.63), kind=kOutput, calls=%fused_computation.7 | convolution fusion | flops 537526272 | bytes 4197376 | tf_op jit(solution)/shard_map/dot_general | solution.py:75
  (22 shorter events, 0.2 us)
Async XLA Ops:
  6.5 1.5 copy-start
  6.5 69.2 %all-gather.5.cloned.1.call-start = ((), (), s32[]{:S(2)}) async-start(), calls=%async_computation.1 | async-start | bytes 4718592 | tf_op jit(solution)/shard_map/all_gather | solution.py:39
  13.2 14.9 %copy-start.3 = (s32[256,5,8]{0,2,1:T(8,128)S(1)}, s32[256,5,8]{0,2,1:T(8,128)}, u32[]{:S(2)}) copy-start(s32[256,5,8]{0,2,1:T(8,128)} %param.11) | copy-start | bytes 122884
  13.2 15.3 %copy-start.5 = (s32[256]{0:T(256)S(1)}, s32[256]{0:T(256)}, u32[]{:S(2)}) copy-start(s32[256]{0:T(256)} %param.9) | copy-start | bytes 3076
  13.4 16.3 %copy-start.4 = (s32[32,5]{0,1:T(8,128)S(1)}, s32[32,5]{0,1:T(8,128)}, u32[]{:S(2)}) copy-start(s32[32,5]{0,1:T(8,128)} %param.10) | copy-start | bytes 1924
  28.0 97.3 %all-gather.7.cloned.1.call-start = ((), (), s32[]{:S(2)}) async-start(), calls=%async_computation.2 | async-start | bytes 2359296 | tf_op jit(solution)/shard_map/all_gather | solution.py:65
  30.8 51.3 %copy-start.2 = (bf16[4,256,256]{1,2,0:T(8,128)(2,1)S(1)}, bf16[4,256,256]{1,2,0:T(8,128)(2,1)}, u32[]{:S(2)}) copy-start(bf16[4,256,256]{1,2,0:T(8,128)(2,1)} %multiply_convert_fusion) | copy-start | bytes 1572868
  90.8 6.1 %copy-start.1 = (f32[256,512]{1,0:T(8,128)S(1)}, f32[256,512]{1,0:T(8,128)}, u32[]{:S(2)}) copy-start(f32[256,512]{1,0:T(8,128)} %param.8) | copy-start | bytes 1572868
  97.8 59.3 %all-gather.9.cloned.1.call-start = ((), (), s32[]{:S(2)}) async-start(), calls=%async_computation.3 | async-start | bytes 2359296 | tf_op jit(solution)/shard_map/all_gather | solution.py:65
  128.4 60.5 %all-gather.11.cloned.1.call-start = ((), (), s32[]{:S(2)}) async-start(), calls=%async_computation.4 | async-start | bytes 2359296 | tf_op jit(solution)/shard_map/all_gather | solution.py:65
Sparse Core Ops, SparseCore 0:
  28.1 47.5 all-gather.4
  98.0 27.3 all-gather.6
  128.5 28.5 all-gather.8
  160.3 28.5 all-gather.10
where the time goes:
time: 199 us
  waiting for transfers between devices  120 us (60%)
  other arithmetic  20.4 us (10%)
  matrix products  17.7 us (9%)
  blocking collectives  13.5 us (7%)
  between operations  13.3 us (7%)
  local copies, waits for them, and re-layouts  12.9 us (6%)
    all_gather x3, waiting for transfers between devices, body(): shard_rows = lax.all_gather(scaled, 'dp', axis=0, tiled=True)  75.5 us
    all_gather x1, waiting for transfers between devices, body(): add_shard_rows = lax.all_gather(unit_rows, 'dp', axis=0, tiled=True)  44.8 us
    all_to_all x1, blocking collectives, body(): lax.all_to_all(cols_part, 'tensor', split_axis=0, concat_axis=1, tiled=True)  13.5 us
    dot_general x3, matrix products, body(): spread = jnp.dot(combined, shard_rows, preferred_element_type=jnp.float32)  9.13 us
    all_gather x1, local copies, waits for them, and re-layouts, body(): add_shard_rows = lax.all_gather(unit_rows, 'dp', axis=0, tiled=True)  6.4 us
    reduce_sum x1, other arithmetic, body(): jnp.sum(jnp.where(onehot_mask, weight_grid[..., None], 0.0), axis=2)  5.58 us
    dot_general x1, matrix products, body(): jnp.dot(embeddings, proj_weight, preferred_element_type=jnp.float32)  5.13 us
    reduce_sum x1, other arithmetic, pick_columns(): jnp.sum(jnp.where(onehot_mask, slot_tiles[:, :, None, :], 0.0), axis=3)  4.66 us
  transfers between devices with their start and end apart: 4, of which 4 were waited for; matrix products, arithmetic and copies ran while one was open for 6% of the time, Pallas kernels for 0%

commit v1 on v0

v1 whole, which is shorter than its diff:
```python
import functools

import jax
import jax.numpy as jnp
from jax import lax
from jax.experimental import pallas as pl
from jax.experimental.pallas import tpu as pltpu
from jax.sharding import PartitionSpec as P

ITERS = 3
CHUNKS = 2
MESH = pl.DeviceIdType.MESH

eps_norm = 1e-06
beta_scale = 16.0
alpha_keep = 0.8


def as_column(row, count):
    return jnp.transpose(jnp.broadcast_to(row, (8, count)))[:, :1]


class Gather:
    def __init__(self, buf, send, recv, groups, me):
        self.buf, self.send, self.recv = buf, send, recv
        self.me, self.core, self.chip = me, lax.rem(me, 2), me // 2
        self.chips = groups // 2
        self.step_rows = buf.shape[1] // CHUNKS

    def copy(self, kind, slot, part, target):
        view = self.buf.at[slot, pl.ds(part * self.step_rows, self.step_rows)]
        return pltpu.make_async_remote_copy(
            src_ref=view,
            dst_ref=view,
            send_sem=self.send.at[kind, slot, part],
            recv_sem=self.recv.at[slot, part],
            device_id={"dp": target},
            device_id_type=MESH,
        )

    def up(self, slot, part):
        return self.copy(0, slot, part, lax.min(self.me + 2, 2 * self.chips - 2 + self.core))

    def down(self, slot, part):
        return self.copy(1, slot, part, lax.max(self.me - 2, self.core))

    def across(self, slot, part):
        return self.copy(2, slot, part, self.chip * 2 + 1 - self.core)

    def begin(self):
        for part in range(CHUNKS):
            @pl.when(self.chip < self.chips - 1)
            def _():
                self.up(self.me, part).start()

            @pl.when(self.chip > 0)
            def _():
                self.down(self.me, part).start()

            self.across(self.me, part).start()

    def from_below(self, dist):
        return self.chip - dist >= 0

    def from_above(self, dist):
        return self.chip + dist < self.chips

    def forward(self, dist):
        for part in range(CHUNKS):
            @pl.when(self.from_below(dist))
            def _():
                slot = self.me - 2 * dist
                self.across(slot, part).wait_recv()

                @pl.when(self.chip < self.chips - 1)
                def _():
                    self.up(slot, part).start()

                self.across(slot, part).start()

            @pl.when(self.from_above(dist))
            def _():
                slot = self.me + 2 * dist
                self.across(slot, part).wait_recv()

                @pl.when(self.chip > 0)
                def _():
                    self.down(slot, part).start()

                self.across(slot, part).start()

    def wait_other(self, slot):
        for part in range(CHUNKS):
            self.across(slot, part).wait_recv()

    def each(self, dist, use):
        for valid, chip in (
            (self.from_below(dist), self.chip - dist),
            (self.from_above(dist), self.chip + dist),
        ):
            @pl.when(valid)
            def _():
                if use is not None:
                    use(chip * 2 + self.core)
                other = chip * 2 + 1 - self.core
                self.wait_other(other)
                if use is not None:
                    use(other)

    def partner_block(self, use):
        other = self.chip * 2 + 1 - self.core
        self.wait_other(other)
        if use is not None:
            use(other)

    def drain(self):
        def one(chip, carry):
            slot = chip * 2 + self.core
            for part in range(CHUNKS):
                @pl.when((chip <= self.chip) & (self.chip < self.chips - 1))
                def _():
                    self.up(slot, part).wait_send()

                @pl.when((chip >= self.chip) & (self.chip > 0))
                def _():
                    self.down(slot, part).wait_send()

                self.across(slot, part).wait_send()
            return carry

        lax.fori_loop(0, self.chips, one, 0)


def kernel(
    groups, panels,
    emb_hbm, weight_hbm, prior_ref, mask_ref, nbr_ref, cols_ref,
    out_ref,
    emb, weight, made, panel, units, seed_blocks, scaled_a, scaled_b, roots, counts, aff, seeds, acc, degree,
    load_sem, a2a_send, a2a_recv, root_send, root_recv,
    u_send, u_recv, s_send, s_recv, a_send, a_recv, b_send, b_recv,
):
    me = lax.axis_index("dp")
    tensor = lax.axis_index("tensor")
    rows = prior_ref.shape[0]
    width = weight.shape[1]
    slots = cols_ref.shape[0]
    picks = cols_ref.shape[1]

    def panel_of(step):
        return lax.rem(tensor + step, panels)

    def load(step):
        span = pl.ds(pl.multiple_of(panel_of(step) * rows, rows), rows)
        return pltpu.make_async_copy(emb_hbm.at[span], emb.at[span], load_sem.at[step])

    weight_copy = pltpu.make_async_copy(weight_hbm, weight, load_sem.at[panels])
    weight_copy.start()
    for step in range(1, panels + 1):
        load(step % panels).start()

    barrier = pltpu.get_barrier_semaphore()
    for step in range(1, groups):
        pl.semaphore_signal(
            barrier, inc=1, device_id={"dp": lax.rem(me + step, groups)}, device_id_type=MESH
        )
    for step in range(1, panels):
        pl.semaphore_signal(barrier, inc=1, device_id={"tensor": panel_of(step)}, device_id_type=MESH)

    prior = prior_ref[...]
    mask = as_column(mask_ref[...].astype(jnp.float32), rows)
    seeds[...] = mask * prior / jnp.mean(prior, axis=1, keepdims=True)
    seed_blocks[me] = seeds[...].astype(jnp.bfloat16)
    pl.semaphore_wait(barrier, groups + panels - 2)

    seed_gather = Gather(seed_blocks, s_send, s_recv, groups, me)
    unit_gather = Gather(units, u_send, u_recv, groups, me)
    seed_gather.begin()

    def a2a(step):
        return pltpu.make_async_remote_copy(
            src_ref=made.at[step],
            dst_ref=panel.at[tensor],
            send_sem=a2a_send.at[step],
            recv_sem=a2a_recv.at[tensor],
            device_id={"tensor": panel_of(step)},
            device_id_type=MESH,
        )

    def project(step):
        load(step).wait()
        span = pl.ds(pl.multiple_of(panel_of(step) * rows, rows), rows)
        return jnp.dot(emb[span], weight[...], preferred_element_type=jnp.float32).astype(jnp.bfloat16)

    weight_copy.wait()

    def project_and_send(step, carry):
        made[step] = project(step)
        a2a(step).start()
        return carry

    lax.fori_loop(1, panels, project_and_send, 0)
    panel[tensor] = project(0)
    seed_gather.forward(1)
    for step in range(1, panels):
        source = panel_of(step)
        pltpu.make_async_remote_copy(
            src_ref=made.at[step],
            dst_ref=panel.at[source],
            send_sem=a2a_send.at[step],
            recv_sem=a2a_recv.at[source],
            device_id={"tensor": source},
            device_id_type=MESH,
        ).wait_recv()
    total = jnp.zeros((rows, 1), jnp.float32)
    for part in range(panels):
        values = panel[part].astype(jnp.float32)
        total += jnp.sum(values * values, axis=1, keepdims=True)
    scale = lax.rsqrt(total + eps_norm)
    for part in range(panels):
        units[me, :, part * width:(part + 1) * width] = (
            panel[part].astype(jnp.float32) * scale
        ).astype(jnp.bfloat16)
    unit_gather.begin()

    ids = lax.broadcasted_iota(jnp.int32, (rows, rows), 0)

    def count(slot, carry):
        chosen = jnp.zeros((picks, rows), jnp.int32) - 1
        for s in range(slots):
            match = (nbr_ref[me * panels + tensor, s] == slot * panels + tensor).astype(jnp.int32)
            chosen += match * (cols_ref[s] + 1)
        number = jnp.zeros((rows, rows), jnp.float32)
        for k in range(picks):
            number += jnp.where(ids == chosen[k:k + 1, :], 1.0, 0.0)
        counts[slot] = number
        return carry

    lax.fori_loop(0, groups, count, 0)
    degree[...] = jnp.zeros_like(degree)

    def seed_step(dist, carry):
        seed_gather.forward(dist)
        return carry

    lax.fori_loop(2, groups // 2, seed_step, 0)

    def affinity(slot):
        tile = lax.dot_general(
            units[slot], units[me], (((1,), (1,)), ((), ())), preferred_element_type=jnp.float32
        )
        number = counts[slot]
        grown = jnp.where(number > 0.0, number * jnp.exp(beta_scale * tile), 0.0)
        degree[...] += jnp.sum(grown, axis=0, keepdims=True)
        aff[slot] = jnp.transpose(grown).astype(jnp.bfloat16)

    unit_gather.partner_block(affinity)

    def unit_step(dist, carry):
        unit_gather.forward(dist)
        unit_gather.each(dist, affinity)
        return carry

    lax.fori_loop(1, groups // 2, unit_step, 0)

    root_row = lax.rsqrt(degree[...])
    roots[me] = jnp.broadcast_to(root_row, (8, rows))

    def root_copy(step, target, slot):
        return pltpu.make_async_remote_copy(
            src_ref=roots.at[slot],
            dst_ref=roots.at[slot],
            send_sem=root_send.at[step],
            recv_sem=root_recv.at[slot],
            device_id={"dp": target},
            device_id_type=MESH,
        )

    for step in range(1, groups):
        root_copy(step, lax.rem(me + step, groups), me).start()
    root = as_column(root_row, rows)
    seed_gather.partner_block(None)

    def seed_rest(dist, carry):
        seed_gather.each(dist, None)
        return carry

    lax.fori_loop(1, groups // 2, seed_rest, 0)
    acc[...] = jnp.zeros_like(acc)

    def first_spread(step, carry):
        slot = lax.rem(me + step, groups)
        root_copy(step, slot, slot).wait_recv()
        near = jnp.transpose(roots[slot])[:, :1]
        scaled = (seed_blocks[slot].astype(jnp.float32) * near).astype(jnp.bfloat16)
        acc[...] += jnp.dot(aff[slot], scaled, preferred_element_type=jnp.float32)
        return carry

    lax.fori_loop(1, groups, first_spread, 0)
    keep = alpha_keep * root

    gathers = []
    for held, send, recv in ((scaled_a, a_send, a_recv), (scaled_b, b_send, b_recv)):
        labels = keep * acc[...] + (1.0 - alpha_keep) * seeds[...]
        held[me] = (labels * root).astype(jnp.bfloat16)
        gather = Gather(held, send, recv, groups, me)
        gather.begin()
        gathers.append(gather)
        acc[...] = jnp.zeros_like(acc)

        def spread(slot, held=held):
            acc[...] += jnp.dot(aff[slot], held[slot], preferred_element_type=jnp.float32)

        gather.partner_block(spread)

        def label_step(dist, carry, gather=gather, spread=spread):
            gather.forward(dist)
            gather.each(dist, spread)
            return carry

        lax.fori_loop(1, groups // 2, label_step, 0)
    out_ref[...] = keep * acc[...] + (1.0 - alpha_keep) * seeds[...]

    for step in range(1, panels):
        a2a(step).wait_send()
    for step in range(1, groups):
        root_copy(step, lax.rem(me + step, groups), me).wait_send()
    for gather in (seed_gather, unit_gather, *gathers):
        gather.drain()


def body(embeddings, proj_weight, class_prior, seed_mask, nbr_block, nbr_cols):
    groups, panels = lax.axis_size("dp"), lax.axis_size("tensor")
    rows, classes = class_prior.shape
    depth, width = proj_weight.shape
    features = width * panels
    cols = jnp.transpose(nbr_cols, (1, 2, 0))
    vmem = pl.BlockSpec(memory_space=pltpu.VMEM)
    anywhere = pl.BlockSpec(memory_space=pl.ANY)
    dma = pltpu.SemaphoreType.DMA
    gather_sems = [dma((3, groups, CHUNKS)), dma((groups, CHUNKS))]
    return pl.pallas_call(
        functools.partial(kernel, groups, panels),
        out_shape=jax.ShapeDtypeStruct((rows, classes), jnp.float32),
        in_specs=[anywhere, anywhere, vmem, vmem, pl.BlockSpec(memory_space=pltpu.SMEM), vmem],
        out_specs=vmem,
        scratch_shapes=[
            pltpu.VMEM(embeddings.shape, jnp.bfloat16),
            pltpu.VMEM(proj_weight.shape, jnp.bfloat16),
            pltpu.VMEM((panels, rows, width), jnp.bfloat16),
            pltpu.VMEM((panels, rows, width), jnp.bfloat16),
            pltpu.VMEM((groups, rows, features), jnp.bfloat16),
            pltpu.VMEM((groups, rows, classes), jnp.bfloat16),
            pltpu.VMEM((groups, rows, classes), jnp.bfloat16),
            pltpu.VMEM((groups, rows, classes), jnp.bfloat16),
            pltpu.VMEM((groups, 8, rows), jnp.float32),
            pltpu.VMEM((groups, rows, rows), jnp.float32),
            pltpu.VMEM((groups, rows, rows), jnp.bfloat16),
            pltpu.VMEM((rows, classes), jnp.float32),
            pltpu.VMEM((rows, classes), jnp.float32),
            pltpu.VMEM((1, rows), jnp.float32),
            dma((panels + 1,)),
            dma((panels,)),
            dma((panels,)),
            dma((groups,)),
            dma((groups,)),
        ] + gather_sems * 4,
        compiler_params=pltpu.CompilerParams(
            collective_id=0, has_side_effects=True, vmem_limit_bytes=60 * 1024 * 1024
        ),
        cost_estimate=pl.CostEstimate(
            flops=2 * rows * panels * depth * width, bytes_accessed=10 << 20, transcendentals=0
        ),
    )(embeddings, proj_weight, class_prior, seed_mask.reshape(1, rows), nbr_block, cols)


def solution(mesh):
    return jax.shard_map(
        body,
        mesh=mesh,
        in_specs=(
            P("dp", None),
            P(None, "tensor"),
            P(("dp", "tensor"), None),
            P(("dp", "tensor")),
            P(),
            P(("dp", "tensor"), None, None),
        ),
        out_specs=P(("dp", "tensor"), None),
        check_vma=False,
    )
```

time: 199 us -> 112 us (0.56)
  waiting for transfers between devices: 120 us -> 0 us
  Pallas kernels: 0 us -> 109 us
  other arithmetic: 20.4 us -> 0 us
  matrix products: 17.7 us -> 0 us
  blocking collectives: 13.5 us -> 0 us
  between operations: 13.3 us -> 0.01 us
  local copies, waits for them, and re-layouts: 12.9 us -> 3.24 us
    all_gather x4 -> x0, waiting for transfers between devices: 120 us -> none  [the longest x3 75.5 us: body(): shard_rows = lax.all_gather(scaled, 'dp', axis=0, tiled=True)]
    pallas_call x0 -> x1, Pallas kernels: none -> 109 us  [body(): pl.pallas_call(functools.partial(kernel, groups, panels), out_shape=jax.S...]
    dot_general x5 -> x0, matrix products: 17.7 us -> none  [the longest x3 9.13 us: body(): spread = jnp.dot(combined, shard_rows, preferred_element_type=jnp.float32)]
    reduce_sum x7 -> x0, other arithmetic: 17.4 us -> none  [the longest x1 5.58 us: body(): jnp.sum(jnp.where(onehot_mask, weight_grid[..., None], 0.0), axis=2)]
    all_to_all x1 -> x0, blocking collectives: 13.5 us -> none  [body(): lax.all_to_all(cols_part, 'tensor', split_axis=0, concat_axis=1, tiled=True)]
    all_gather x1 -> x0, local copies, waits for them, and re-layouts: 6.4 us -> none  [body(): add_shard_rows = lax.all_gather(unit_rows, 'dp', axis=0, tiled=True)]
    convert_element_type x4 -> x0, other arithmetic: 2.67 us -> none  [the longest x2 1.79 us: body(): unit_rows = (panel_f * lax.rsqrt(jnp.sum(panel_f * panel_f, axis=1, keepd...]
  transfers between devices with their start and end apart: 4 -> 0, of which waited for: 4 -> 0; matrix products, arithmetic and copies ran while one was open for 6% -> 0% of each run, Pallas kernels for 0% -> 0%
where the time goes in v1:
time: 112 us
  Pallas kernels  109 us (97%)
  local copies, waits for them, and re-layouts  3.24 us (3%)
    pallas_call x1, Pallas kernels, body(): pl.pallas_call(functools.partial(kernel, groups, panels), out_shape=jax.S...  109 us
    unnamed x2, local copies, waits for them, and re-layouts  3.24 us

profile of v1, /device:TPU:0, one launch (start us, length us, event | category | flops | bytes accessed | tf_op | source)
XLA Modules:
  0.0 112.1 jit_solution(7971842194999856666)
XLA Ops:
  0.0 1.4 %copy.7.nbr_ref = s32[32,5]{1,0:T(8,128)} copy(s32[32,5]{0,1:T(8,128)} %param.10) | data formatting | bytes 1280 | tf_op args[4]
  1.4 108.8 %shard_map.64 = f32[256,512]{1,0:T(8,128)} custom-call(bf16[1024,3584]{1,0:T(8,128)(2,1)} %emb_hbm.1, bf16[3584,256]{1,0:T(8,128)(2,1)} %weight_hbm.1, f32[256,512]{1,0:T(8,128)} %prior_ref.1, s32[1,256]{1,0:T(1,128)} %bitcast.3, s32[32,5]{1,0:T(8,128)} %copy.7.nbr_ref, s32[5,8,256]{2,1,0:T(8,128)} %bitcast.2), custom_call_target="tpu_custom_call" | custom-call | flops 1879048192 | bytes 10485760 | tf_op jit(solution)/shard_map/pallas_call | solution.py:341
  110.2 1.9 %copy.9 = f32[256,512]{1,0:T(8,128)} copy(f32[256,512]{1,0:T(8,128)} %shard_map.64) | data formatting | bytes 1048576

commit v2 on v1

v2 whole, which is shorter than its diff:
```python
import functools

import jax
import jax.numpy as jnp
from jax import lax
from jax.experimental import pallas as pl
from jax.experimental.pallas import tpu as pltpu
from jax.sharding import PartitionSpec as P

ITERS = 3
CHUNKS = 2
PIECES = 2
MESH = pl.DeviceIdType.MESH

eps_norm = 1e-06
beta_scale = 16.0
alpha_keep = 0.8


def as_column(row, count):
    return jnp.transpose(jnp.broadcast_to(row, (8, count)))[:, :1]


class Gather:
    def __init__(self, buf, send, recv, groups, me, inner, parts=CHUNKS):
        self.buf, self.send, self.recv, self.parts = buf, send, recv, parts
        self.me, self.core, self.chip = me, lax.rem(me, 2), me // 2
        self.chips = groups // 2
        self.inner = inner
        self.step_rows = buf.shape[1] // parts
        self.is_inner = (self.chip >= 1) & (self.chip <= self.chips - 2)
        self.can_up = self.chip <= self.chips - 3
        self.can_down = self.chip >= 2
        if inner:
            self.can_up = self.can_up & self.is_inner
            self.can_down = self.can_down & self.is_inner

    def copy(self, kind, slot, part, target):
        view = self.buf.at[slot, pl.ds(part * self.step_rows, self.step_rows)]
        return pltpu.make_async_remote_copy(
            src_ref=view,
            dst_ref=view,
            send_sem=self.send.at[kind, slot, part],
            recv_sem=self.recv.at[slot, part],
            device_id={"dp": target},
            device_id_type=MESH,
        )

    def up(self, slot, part):
        return self.copy(0, slot, part, lax.min(self.me + 2, 2 * self.chips - 2 + self.core))

    def down(self, slot, part):
        return self.copy(1, slot, part, lax.max(self.me - 2, self.core))

    def across(self, slot, part):
        return self.copy(2, slot, part, self.chip * 2 + 1 - self.core)

    def pass_on(self, slot, part, upward, downward):
        if upward:
            @pl.when(self.can_up)
            def _():
                self.up(slot, part).start()
        if downward:
            @pl.when(self.can_down)
            def _():
                self.down(slot, part).start()

        @pl.when(self.is_inner)
        def _():
            self.across(slot, part).start()

    def begin(self):
        for part in range(self.parts):
            self.pass_on(self.me, part, True, True)
        if self.inner:
            for part in range(self.parts):
                @pl.when(self.chip == 1)
                def _():
                    self.pass_on(self.me - 2, part, True, False)

                @pl.when(self.chip == self.chips - 2)
                def _():
                    self.pass_on(self.me + 2, part, False, True)

    def from_below(self, dist):
        return self.is_inner & (self.chip - dist >= 0)

    def from_above(self, dist):
        return self.is_inner & (self.chip + dist < self.chips)

    def arrives(self, dist):
        below, above = self.from_below(dist), self.from_above(dist)
        if self.inner:
            below = below & ((self.chip > 1) | (dist > 1))
            above = above & ((self.chip < self.chips - 2) | (dist > 1))
        return below, above

    def forward(self, dist):
        below, above = self.arrives(dist)
        for part in range(self.parts):
            @pl.when(below)
            def _():
                slot = self.me - 2 * dist
                self.across(slot, part).wait_recv()
                self.pass_on(slot, part, True, False)

            @pl.when(above)
            def _():
                slot = self.me + 2 * dist
                self.across(slot, part).wait_recv()
                self.pass_on(slot, part, False, True)

    def wait_other(self, slot):
        for part in range(self.parts):
            self.across(slot, part).wait_recv()

    def each(self, dist, use):
        for valid, chip in (
            (self.from_below(dist), self.chip - dist),
            (self.from_above(dist), self.chip + dist),
        ):
            @pl.when(valid)
            def _():
                if use is not None:
                    use(chip * 2 + self.core)
                other = chip * 2 + 1 - self.core
                self.wait_other(other)
                if use is not None:
                    use(other)

    def own_chip(self, use):
        @pl.when(self.is_inner)
        def _():
            other = self.chip * 2 + 1 - self.core
            if use is not None:
                use(self.me)
            self.wait_other(other)
            if use is not None:
                use(other)

    def receive(self, use, begin=1):
        self.own_chip(use)

        def step(dist, carry):
            self.forward(dist)
            self.each(dist, use)
            return carry

        lax.fori_loop(begin, self.chips - 1, step, 0)

    def drain(self):
        def one(chip, carry):
            slot = chip * 2 + self.core
            for part in range(self.parts):
                @pl.when((chip <= self.chip) & self.can_up)
                def _():
                    self.up(slot, part).wait_send()

                @pl.when((chip >= self.chip) & self.can_down)
                def _():
                    self.down(slot, part).wait_send()

                @pl.when(self.is_inner)
                def _():
                    self.across(slot, part).wait_send()
            return carry

        lax.fori_loop(0, self.chips, one, 0)


def kernel(
    groups, panels,
    emb_hbm, weight_hbm, prior_ref, mask_ref, nbr_ref, cols_ref,
    out_ref,
    emb, weight, made, panel, units, seed_blocks, scaled_a, scaled_b, roots, counts, aff, seeds, acc, degree,
    far_cols, back,
    load_sem, a2a_send, a2a_recv, far_send, far_recv, back_send, back_recv,
    u_send, u_recv, s_send, s_recv, a_send, a_recv, b_send, b_recv, r_send, r_recv,
):
    me = lax.axis_index("dp")
    tensor = lax.axis_index("tensor")
    rows = prior_ref.shape[0]
    width = weight.shape[1]
    slots = cols_ref.shape[0]
    picks = cols_ref.shape[1]

    def panel_of(step):
        return lax.rem(tensor + step, panels)

    def load(step):
        span = pl.ds(pl.multiple_of(panel_of(step) * rows, rows), rows)
        return pltpu.make_async_copy(emb_hbm.at[span], emb.at[span], load_sem.at[step])

    weight_copy = pltpu.make_async_copy(weight_hbm, weight, load_sem.at[panels])
    weight_copy.start()
    for step in range(1, panels + 1):
        load(step % panels).start()

    barrier = pltpu.get_barrier_semaphore()
    for step in range(1, groups):
        pl.semaphore_signal(
            barrier, inc=1, device_id={"dp": lax.rem(me + step, groups)}, device_id_type=MESH
        )
    for step in range(1, panels):
        pl.semaphore_signal(barrier, inc=1, device_id={"tensor": panel_of(step)}, device_id_type=MESH)

    prior = prior_ref[...]
    mask = as_column(mask_ref[...].astype(jnp.float32), rows)
    seeds[...] = mask * prior / jnp.mean(prior, axis=1, keepdims=True)
    seed_blocks[me] = seeds[...].astype(jnp.bfloat16)
    pl.semaphore_wait(barrier, groups + panels - 2)

    chip, chips, core = me // 2, groups // 2, lax.rem(me, 2)
    is_inner = (chip >= 1) & (chip <= chips - 2)
    is_outer = (chip == 0) | (chip == chips - 1)
    has_far = (chip == 1) | (chip == chips - 2)
    partner = jnp.where(chip == 0, 2 + core, 2 * chips - 4 + core)
    far = jnp.where(chip == 1, core, 2 * chips - 2 + core)

    seed_gather = Gather(seed_blocks, s_send, s_recv, groups, me, False)
    unit_gather = Gather(units, u_send, u_recv, groups, me, False)
    cols_copy = pltpu.make_async_remote_copy(
        src_ref=cols_ref,
        dst_ref=far_cols,
        send_sem=far_send,
        recv_sem=far_recv,
        device_id={"dp": partner},
        device_id_type=MESH,
    )

    @pl.when(is_outer)
    def _():
        cols_copy.start()

    seed_gather.begin()

    def a2a(step):
        return pltpu.make_async_remote_copy(
            src_ref=made.at[step],
            dst_ref=panel.at[tensor],
            send_sem=a2a_send.at[step],
            recv_sem=a2a_recv.at[tensor],
            device_id={"tensor": panel_of(step)},
            device_id_type=MESH,
        )

    def project(step):
        load(step).wait()
        span = pl.ds(pl.multiple_of(panel_of(step) * rows, rows), rows)
        return jnp.dot(emb[span], weight[...], preferred_element_type=jnp.float32).astype(jnp.bfloat16)

    weight_copy.wait()

    def project_and_send(step, carry):
        made[step] = project(step)
        a2a(step).start()
        return carry

    lax.fori_loop(1, panels, project_and_send, 0)
    panel[tensor] = project(0)
    seed_gather.forward(1)
    for step in range(1, panels):
        source = panel_of(step)
        pltpu.make_async_remote_copy(
            src_ref=made.at[step],
            dst_ref=panel.at[source],
            send_sem=a2a_send.at[step],
            recv_sem=a2a_recv.at[source],
            device_id={"tensor": source},
            device_id_type=MESH,
        ).wait_recv()
    total = jnp.zeros((rows, 1), jnp.float32)
    for part in range(panels):
        values = panel[part].astype(jnp.float32)
        total += jnp.sum(values * values, axis=1, keepdims=True)
    scale = lax.rsqrt(total + eps_norm)
    for part in range(panels):
        units[me, :, part * width:(part + 1) * width] = (
            panel[part].astype(jnp.float32) * scale
        ).astype(jnp.bfloat16)
    unit_gather.begin()

    ids = lax.broadcasted_iota(jnp.int32, (rows, rows), 0)

    def owners(use):
        use(0, me, cols_ref)

        @pl.when(has_far)
        def _():
            use(1, far, far_cols)

    def count_for(which, owner, cols):
        def count(slot, carry):
            chosen = jnp.zeros((picks, rows), jnp.int32) - 1
            for s in range(slots):
                match = (nbr_ref[owner * panels + tensor, s] == slot * panels + tensor).astype(jnp.int32)
                chosen += match * (cols[s] + 1)
            number = jnp.zeros((rows, rows), jnp.float32)
            for k in range(picks):
                number += jnp.where(ids == chosen[k:k + 1, :], 1.0, 0.0)
            counts[which, slot] = number
            return carry

        lax.fori_loop(0, groups, count, 0)

    seed_gather.forward(2)

    @pl.when(is_inner)
    def _():
        @pl.when(has_far)
        def _():
            cols_copy.wait_recv()

        owners(count_for)

    degree[...] = jnp.zeros_like(degree)

    def seed_step(dist, carry):
        seed_gather.forward(dist)
        return carry

    lax.fori_loop(3, chips - 1, seed_step, 0)

    def affinity(slot):
        def one(which, owner, cols):
            tile = lax.dot_general(
                units[slot], units[owner], (((1,), (1,)), ((), ())), preferred_element_type=jnp.float32
            )
            number = counts[which, slot]
            grown = jnp.where(number > 0.0, number * jnp.exp(beta_scale * tile), 0.0)
            degree[which] += jnp.sum(grown, axis=0, keepdims=True)
            aff[which, slot] = jnp.transpose(grown).astype(jnp.bfloat16)

        owners(one)

    unit_gather.forward(1)
    unit_gather.own_chip(affinity)
    unit_gather.each(1, affinity)

    def unit_step(dist, carry):
        unit_gather.forward(dist)
        unit_gather.each(dist, affinity)
        return carry

    lax.fori_loop(2, chips - 1, unit_step, 0)
    gathers = [seed_gather, unit_gather]

    def seed_rest(dist, carry):
        seed_gather.each(dist, None)
        return carry

    seed_gather.own_chip(None)
    lax.fori_loop(1, chips - 1, seed_rest, 0)

    def column_of(slot):
        return jnp.transpose(roots[slot])[:, :1]

    def add_spread(slot, near, first, width):
        def one(which, owner, cols):
            acc[which, :, first:first + width] += jnp.dot(
                aff[which, slot], near, preferred_element_type=jnp.float32
            )

        owners(one)

    @pl.when(is_inner)
    def _():
        def set_root(which, owner, cols):
            roots[owner] = jnp.broadcast_to(lax.rsqrt(degree[which]), (8, rows))

        owners(set_root)

    root_gather = Gather(roots, r_send, r_recv, groups, me, True, 1)
    root_gather.begin()
    gathers.append(root_gather)
    acc[...] = jnp.zeros_like(acc)
    classes = prior_ref.shape[1]

    def first_spread(slot):
        scaled = (seed_blocks[slot].astype(jnp.float32) * column_of(slot)).astype(jnp.bfloat16)
        add_spread(slot, scaled, 0, classes)

    root_gather.receive(first_spread)

    def mix(first, width):
        def one(which, owner, cols):
            root = column_of(owner)
            if which == 0:
                kept = seeds[:, first:first + width]
            else:
                kept = seed_blocks[owner, :, first:first + width].astype(jnp.float32)
            labels = alpha_keep * root * acc[which, :, first:first + width] + (1.0 - alpha_keep) * kept
            held[owner] = (labels * root).astype(jnp.bfloat16)

        owners(one)

    held = scaled_a
    pl.when(is_inner)(lambda: mix(0, classes))
    acc[...] = jnp.zeros_like(acc)
    gather = Gather(scaled_a, a_send, a_recv, groups, me, True)
    gather.begin()
    gathers.append(gather)
    gather.receive(lambda slot: add_spread(slot, scaled_a[slot], 0, classes))

    piece = classes // PIECES
    last = []
    for part in range(PIECES):
        held = scaled_b.at[part]
        pl.when(is_inner)(lambda: mix(part * piece, piece))
        gather = Gather(held, b_send.at[part], b_recv.at[part], groups, me, True)
        gather.begin()
        last.append(gather)
    gathers += last
    acc[...] = jnp.zeros_like(acc)

    def back_copy(part, target):
        return pltpu.make_async_remote_copy(
            src_ref=back.at[part],
            dst_ref=back.at[part],
            send_sem=back_send.at[part],
            recv_sem=back_recv.at[part],
            device_id={"dp": target},
            device_id_type=MESH,
        )

    for part in range(PIECES):
        near_blocks = scaled_b.at[part]
        last[part].receive(lambda slot: add_spread(slot, near_blocks[slot], part * piece, piece))

        @pl.when(has_far)
        def _():
            back[part] = alpha_keep * column_of(far) * acc[1, :, part * piece:(part + 1) * piece]
            back_copy(part, far).start()

        @pl.when(is_inner)
        def _():
            back_kept = alpha_keep * column_of(me) * acc[0, :, part * piece:(part + 1) * piece]
            out_ref[:, part * piece:(part + 1) * piece] = (
                back_kept + (1.0 - alpha_keep) * seeds[:, part * piece:(part + 1) * piece]
            )

        @pl.when(is_outer)
        def _():
            back_copy(part, partner).wait_recv()
            out_ref[:, part * piece:(part + 1) * piece] = (
                back[part] + (1.0 - alpha_keep) * seeds[:, part * piece:(part + 1) * piece]
            )

    @pl.when(is_outer)
    def _():
        cols_copy.wait_send()

    @pl.when(has_far)
    def _():
        for part in range(PIECES):
            back_copy(part, far).wait_send()

    for step in range(1, panels):
        a2a(step).wait_send()
    for gather in gathers:
        gather.drain()


def body(embeddings, proj_weight, class_prior, seed_mask, nbr_block, nbr_cols):
    groups, panels = lax.axis_size("dp"), lax.axis_size("tensor")
    rows, classes = class_prior.shape
    depth, width = proj_weight.shape
    features = width * panels
    cols = jnp.transpose(nbr_cols, (1, 2, 0))
    vmem = pl.BlockSpec(memory_space=pltpu.VMEM)
    anywhere = pl.BlockSpec(memory_space=pl.ANY)
    dma = pltpu.SemaphoreType.DMA
    gather_sems = [dma((3, groups, CHUNKS)), dma((groups, CHUNKS))]
    return pl.pallas_call(
        functools.partial(kernel, groups, panels),
        out_shape=jax.ShapeDtypeStruct((rows, classes), jnp.float32),
        in_specs=[anywhere, anywhere, vmem, vmem, pl.BlockSpec(memory_space=pltpu.SMEM), vmem],
        out_specs=vmem,
        scratch_shapes=[
            pltpu.VMEM(embeddings.shape, jnp.bfloat16),
            pltpu.VMEM(proj_weight.shape, jnp.bfloat16),
            pltpu.VMEM((panels, rows, width), jnp.bfloat16),
            pltpu.VMEM((panels, rows, width), jnp.bfloat16),
            pltpu.VMEM((groups, rows, features), jnp.bfloat16),
            pltpu.VMEM((groups, rows, classes), jnp.bfloat16),
            pltpu.VMEM((groups, rows, classes), jnp.bfloat16),
            pltpu.VMEM((PIECES, groups, rows, classes // PIECES), jnp.bfloat16),
            pltpu.VMEM((groups, 8, rows), jnp.float32),
            pltpu.VMEM((2, groups, rows, rows), jnp.float32),
            pltpu.VMEM((2, groups, rows, rows), jnp.bfloat16),
            pltpu.VMEM((rows, classes), jnp.float32),
            pltpu.VMEM((2, rows, classes), jnp.float32),
            pltpu.VMEM((2, 1, rows), jnp.float32),
            pltpu.VMEM(cols.shape, jnp.int32),
            pltpu.VMEM((PIECES, rows, classes // PIECES), jnp.float32),
            dma((panels + 1,)),
            dma((panels,)),
            dma((panels,)),
            dma(()),
            dma(()),
            dma((PIECES,)),
            dma((PIECES,)),
        ] + gather_sems * 3 + [
            dma((PIECES, 3, groups, CHUNKS)),
            dma((PIECES, groups, CHUNKS)),
            dma((3, groups, 1)),
            dma((groups, 1)),
        ],
        compiler_params=pltpu.CompilerParams(
            collective_id=0, has_side_effects=True, vmem_limit_bytes=60 * 1024 * 1024
        ),
        cost_estimate=pl.CostEstimate(
            flops=2 * rows * panels * depth * width, bytes_accessed=10 << 20, transcendentals=0
        ),
    )(embeddings, proj_weight, class_prior, seed_mask.reshape(1, rows), nbr_block, cols)


def solution(mesh):
    return jax.shard_map(
        body,
        mesh=mesh,
        in_specs=(
            P("dp", None),
            P(None, "tensor"),
            P(("dp", "tensor"), None),
            P(("dp", "tensor")),
            P(),
            P(("dp", "tensor"), None, None),
        ),
        out_specs=P(("dp", "tensor"), None),
        check_vma=False,
    )
```

time: 112 us -> 97.2 us (0.87)
  Pallas kernels: 109 us -> 93.7 us
    pallas_call x1, Pallas kernels: 109 us -> 93.7 us  [body(): pl.pallas_call(functools.partial(kernel, groups, panels), out_shape=jax.S...]
where the time goes in v2:
time: 97.2 us; the launch traced here: 96.9 us
  Pallas kernels  93.7 us (96%)
  local copies, waits for them, and re-layouts  3.24 us (3%)
    pallas_call x1, Pallas kernels, body(): pl.pallas_call(functools.partial(kernel, groups, panels), out_shape=jax.S...  93.7 us
    unnamed x2, local copies, waits for them, and re-layouts  3.24 us

profile of v2, /device:TPU:0, one launch (start us, length us, event | category | flops | bytes accessed | tf_op | source)
XLA Modules:
  0.0 96.9 jit_solution(543531880597741551)
XLA Ops:
  0.0 1.4 %copy.7.nbr_ref = s32[32,5]{1,0:T(8,128)} copy(s32[32,5]{0,1:T(8,128)} %param.10) | data formatting | bytes 1280 | tf_op args[4]
  1.4 93.7 %shard_map.64 = f32[256,512]{1,0:T(8,128)} custom-call(bf16[1024,3584]{1,0:T(8,128)(2,1)} %emb_hbm.1, bf16[3584,256]{1,0:T(8,128)(2,1)} %weight_hbm.1, f32[256,512]{1,0:T(8,128)} %prior_ref.1, s32[1,256]{1,0:T(1,128)} %bitcast.3, s32[32,5]{1,0:T(8,128)} %copy.7.nbr_ref, s32[5,8,256]{2,1,0:T(8,128)} %bitcast.2), custom_call_target="tpu_custom_call" | custom-call | flops 1879048192 | bytes 10485760 | tf_op jit(solution)/shard_map/pallas_call | solution.py:474
  95.1 1.9 %copy.9 = f32[256,512]{1,0:T(8,128)} copy(f32[256,512]{1,0:T(8,128)} %shard_map.64) | data formatting | bytes 1048576

commit v3 on v2

--- a/solution.py
+++ b/solution.py
@@ -376,13 +376,9 @@
     acc[...] = jnp.zeros_like(acc)
     classes = prior_ref.shape[1]
 
-    def first_spread(slot):
-        scaled = (seed_blocks[slot].astype(jnp.float32) * column_of(slot)).astype(jnp.bfloat16)
-        add_spread(slot, scaled, 0, classes)
-
-    root_gather.receive(first_spread)
-
-    def mix(first, width):
+    piece = classes // PIECES
+
+    def mix(first, width, held):
         def one(which, owner, cols):
             root = column_of(owner)
             if which == 0:
@@ -391,27 +387,42 @@
                 kept = seed_blocks[owner, :, first:first + width].astype(jnp.float32)
             labels = alpha_keep * root * acc[which, :, first:first + width] + (1.0 - alpha_keep) * kept
             held[owner] = (labels * root).astype(jnp.bfloat16)
+            acc[which, :, first:first + width] = jnp.zeros((rows, width), jnp.float32)
 
         owners(one)
 
-    held = scaled_a
-    pl.when(is_inner)(lambda: mix(0, classes))
-    acc[...] = jnp.zeros_like(acc)
-    gather = Gather(scaled_a, a_send, a_recv, groups, me, True)
-    gather.begin()
-    gathers.append(gather)
-    gather.receive(lambda slot: add_spread(slot, scaled_a[slot], 0, classes))
-
-    piece = classes // PIECES
+    def send_piece(part, blocks, send, recv):
+        held = blocks.at[part]
+        pl.when(is_inner)(lambda: mix(part * piece, piece, held))
+        gather = Gather(held, send.at[part], recv.at[part], groups, me, True)
+        gather.begin()
+        gathers.append(gather)
+        return gather
+
+    second = []
+    for part in range(PIECES):
+        span = slice(part * piece, (part + 1) * piece)
+
+        def first_spread(slot):
+            scaled = (seed_blocks[slot, :, span].astype(jnp.float32) * column_of(slot)).astype(jnp.bfloat16)
+            add_spread(slot, scaled, part * piece, piece)
+
+        if part == 0:
+            root_gather.receive(first_spread)
+        else:
+            @pl.when(is_inner)
+            def _():
+                def rest(slot, carry):
+                    first_spread(slot)
+                    return carry
+
+                lax.fori_loop(0, groups, rest, 0)
+        second.append(send_piece(part, scaled_a, a_send, a_recv))
     last = []
     for part in range(PIECES):
-        held = scaled_b.at[part]
-        pl.when(is_inner)(lambda: mix(part * piece, piece))
-        gather = Gather(held, b_send.at[part], b_recv.at[part], groups, me, True)
-        gather.begin()
-        last.append(gather)
-    gathers += last
-    acc[...] = jnp.zeros_like(acc)
+        near_blocks = scaled_a.at[part]
+        second[part].receive(lambda slot: add_spread(slot, near_blocks[slot], part * piece, piece))
+        last.append(send_piece(part, scaled_b, b_send, b_recv))
 
     def back_copy(part, target):
         return pltpu.make_async_remote_copy(
@@ -483,7 +494,7 @@
             pltpu.VMEM((panels, rows, width), jnp.bfloat16),
             pltpu.VMEM((groups, rows, features), jnp.bfloat16),
             pltpu.VMEM((groups, rows, classes), jnp.bfloat16),
-            pltpu.VMEM((groups, rows, classes), jnp.bfloat16),
+            pltpu.VMEM((PIECES, groups, rows, classes // PIECES), jnp.bfloat16),
             pltpu.VMEM((PIECES, groups, rows, classes // PIECES), jnp.bfloat16),
             pltpu.VMEM((groups, 8, rows), jnp.float32),
             pltpu.VMEM((2, groups, rows, rows), jnp.float32),
@@ -500,7 +511,9 @@
             dma(()),
             dma((PIECES,)),
             dma((PIECES,)),
-        ] + gather_sems * 3 + [
+        ] + gather_sems * 2 + [
+            dma((PIECES, 3, groups, CHUNKS)),
+            dma((PIECES, groups, CHUNKS)),
             dma((PIECES, 3, groups, CHUNKS)),
             dma((PIECES, groups, CHUNKS)),
             dma((3, groups, 1)),

time: 97.2 us -> 93.8 us (0.965)
  Pallas kernels: 93.7 us -> 90.4 us
    pallas_call x1, Pallas kernels: 93.7 us -> 90.4 us  [body(): pl.pallas_call(functools.partial(kernel, groups, panels), out_shape=jax.S...]
where the time goes in v3:
time: 93.8 us; the launch traced here: 93.6 us
  Pallas kernels  90.4 us (96%)
  local copies, waits for them, and re-layouts  3.24 us (3%)
    pallas_call x1, Pallas kernels, body(): pl.pallas_call(functools.partial(kernel, groups, panels), out_shape=jax.S...  90.4 us
    unnamed x2, local copies, waits for them, and re-layouts  3.24 us

profile of v3, /device:TPU:0, one launch (start us, length us, event | category | flops | bytes accessed | tf_op | source)
XLA Modules:
  0.0 93.6 jit_solution(12833048985247116598)
XLA Ops:
  0.0 1.4 %copy.7.nbr_ref = s32[32,5]{1,0:T(8,128)} copy(s32[32,5]{0,1:T(8,128)} %param.10) | data formatting | bytes 1280 | tf_op args[4]
  1.4 90.4 %shard_map.64 = f32[256,512]{1,0:T(8,128)} custom-call(bf16[1024,3584]{1,0:T(8,128)(2,1)} %emb_hbm.1, bf16[3584,256]{1,0:T(8,128)(2,1)} %weight_hbm.1, f32[256,512]{1,0:T(8,128)} %prior_ref.1, s32[1,256]{1,0:T(1,128)} %bitcast.3, s32[32,5]{1,0:T(8,128)} %copy.7.nbr_ref, s32[5,8,256]{2,1,0:T(8,128)} %bitcast.2), custom_call_target="tpu_custom_call" | custom-call | flops 1879048192 | bytes 10485760 | tf_op jit(solution)/shard_map/pallas_call | solution.py:485
  91.8 1.9 %copy.9 = f32[256,512]{1,0:T(8,128)} copy(f32[256,512]{1,0:T(8,128)} %shard_map.64) | data formatting | bytes 1048576
